TPU v7x, 32 devices: a whole 2x2x4 slice. The times are simulated.
32 devices in a mesh: rep: 4 (over z), fsdp: 8 (over y, x, core).
Axes of the slice: x: 2, y: 2, z: 4, core: 2. Of those that a mesh axis runs over, the one named last changes fastest.
Arguments:
- acts: bfloat16 [4, 4096, 3072], P('rep', 'fsdp'), may hold values from -6 to 6
- cotangent: bfloat16 [4, 4096, 512], P('rep', 'fsdp'), may hold values from -0.09375 to 0.09375
- nonfinite_row_mask: int32 [4, 3072], P('rep', 'fsdp'), may hold values from 0 to 1, as said below
- params: float32 [4, 3072, 512], P('rep', 'fsdp'), may hold values from -6 to 6
- adam_first_state: float32 [4, 3072, 512], P('rep', 'fsdp'), may hold values from -6 to 6
- adam_second_state: float32 [4, 3072, 512], P('rep', 'fsdp'), may hold values from 0.2 to 4
- anchor: float32 [3072, 512], P('fsdp'), may hold values from -6 to 6
- momentum: float32 [3072, 512], P('fsdp'), may hold values from -3 to 3
Outputs:
- anchor_next: float32 [3072, 512], P('fsdp')
- momentum_next: float32 [3072, 512], P('fsdp')
- first_next: float32 [4, 3072, 512], P('rep', 'fsdp')
- second_next: float32 [4, 3072, 512], P('rep', 'fsdp')
Inputs may be any that keep to these rules, and one draw needn't show every extreme that they name: `nonfinite_row_mask`: exactly one replica has a marked row, and it has exactly one; all other replicas have none.
All inputs are finite; a program needn't handle non-finite values.
Results may differ from a plain program's by a relative error of at most 0.0003.
Values may be sent and summed in bfloat16 or wider, within the bound.
A program may use at most 128 MiB of HBM per device.

v0:
```python
import jax
import jax.numpy as jnp
from jax import lax
from jax.sharding import PartitionSpec as P

corr_first = 1.0 - 0.9**10
corr_second = 1.0 - 0.95**10


def body(
    acts,
    cotangent,
    nonfinite_row_mask,
    params,
    adam_first_state,
    adam_second_state,
    anchor,
    momentum,
):
    inputs = acts[0]
    upstream = cotangent[0]
    contract = (((0,), (0,)), ((), ()))
    gradient_value = lax.psum_scatter(
        lax.dot_general(inputs, upstream, contract, preferred_element_type=jnp.float32),
        "fsdp",
        scatter_dimension=0,
        tiled=True,
    )
    corrupted_gradient = jnp.where(
        (nonfinite_row_mask[0] == 1)[:, None], jnp.float32(jnp.nan), gradient_value
    )
    replica_nonfinite = jnp.any(jnp.isnan(corrupted_gradient)).astype(jnp.int32)
    first_state_value = 0.9 * adam_first_state[0] + 0.1 * corrupted_gradient
    second_state_value = (
        0.95 * adam_second_state[0] + 0.05 * corrupted_gradient * corrupted_gradient
    )
    update = first_state_value / corr_first / (jnp.sqrt(second_state_value / corr_second) + 1e-08)
    inner = params[0] - 0.1 * (update + 0.1 * params[0])
    pseudo = anchor - inner
    replica_bad = lax.pmax(replica_nonfinite, "fsdp")
    keep = replica_bad == 0
    share = jnp.where(keep, pseudo, jnp.float32(0.0))
    total, count = lax.psum((share, keep.astype(jnp.float32)), "rep")
    average = total / count
    momentum_next = 0.9 * momentum + average
    anchor_next = anchor - 0.7 * (average + 0.9 * momentum_next)
    first_next = jnp.where(keep, first_state_value, adam_first_state[0])[None]
    second_next = jnp.where(keep, second_state_value, adam_second_state[0])[None]
    return (anchor_next, momentum_next, first_next, second_next)


def solution(mesh):
    in_specs = (
        P("rep", "fsdp", None),
        P("rep", "fsdp", None),
        P("rep", "fsdp"),
        P("rep", "fsdp", None),
        P("rep", "fsdp", None),
        P("rep", "fsdp", None),
        P("fsdp", None),
        P("fsdp", None),
    )
    out_specs = (P("fsdp", None), P("fsdp", None), P("rep", "fsdp", None), P("rep", "fsdp", None))
    return jax.shard_map(body, mesh=mesh, in_specs=in_specs, out_specs=out_specs, check_vma=False)
```

profile of v0, /device:TPU:0, one launch (start us, length us, event | category | flops | bytes accessed | tf_op | source)
XLA Modules:
  0.0 149.2 jit_solution(5608221114492774977)
XLA Ops:
  7.2 0.0 copy-start
  7.2 0.0 reduce-scatter.2.cloned.1.call-start
  7.2 1.8 %copy-done = bf16[1,512,3072]{2,1,0:T(8,128)(2,1)S(1)} copy-done((bf16[1,512,3072]{2,1,0:T(8,128)(2,1)S(1)}, bf16[1,512,3072]{2,1,0:T(8,128)(2,1)}, u32[]{:S(2)}) %copy-start) | copy-done | bytes 3145752
  9.1 5.5 %fusion = f32[3072,512]{1,0:T(8,128)} fusion(bf16[1,512,3072]{2,1,0:T(8,128)(2,1)S(1)} %copy-done, bf16[1,512,512]{2,1,0:T(8,128)(2,1)} %param.9), kind=kOutput, calls=%fused_computation | convolution fusion | flops 1610612736 | bytes 9961472 | tf_op jit(solution)/shard_map/dot_general | solution.py:24
  14.6 0.0 copy-start.1
  14.6 0.0 reduce-scatter.2.cloned.1.call-update
  14.6 0.0 all-reduce.2.cloned.1.call-start
  14.7 0.6 copy-done.1
  15.3 63.9 %reduce-scatter.2.cloned.1.call-done = f32[384,512]{1,0:T(8,128)} async-done(((f32[3072,512]{1,0:T(8,128)}), f32[384,512]{1,0:T(8,128)}) %reduce-scatter.2.cloned.1.call-update) | async-done | bytes 786448 | tf_op jit(solution)/shard_map/reduce_scatter | solution.py:23
  79.2 2.0 %compare_reduce_fusion = pred[]{:T(512)} fusion(f32[384,512]{1,0:T(8,128)} %reduce-scatter.2.cloned.1.call-done, pred[384]{0:T(512)(128)(4,1)S(1)} %compare_reduce_fusion.1), kind=kLoop, calls=%fused_computation.19 | loop fusion | flops 589823 | bytes 786817 | tf_op jit(solution)/shard_map/reduce_or | solution.py:32
  81.9 7.8 %pmax.7 = s32[]{:T(128)} all-reduce(s32[]{:T(128)S(6)} %convert_element_type.6), channel_id=1, replica_groups=mesh['rep'=4,'fsdp'=8] {'fsdp'}, use_global_device_ids=true, to_apply=%region_2.3 | all-reduce | flops 1 | bytes 8 | tf_op jit(solution)/shard_map/pmax | solution.py:40
  90.3 4.5 %fusion.3 = (f32[1,384,512]{2,1,0:T(8,128)}, f32[384,512]{1,0:T(8,128)}, f32[1,384,512]{2,1,0:T(8,128)}) fusion(f32[1,384,512]{2,1,0:T(8,128)} %param.13, f32[384,512]{1,0:T(8,128)} %reduce-scatter.2.cloned.1.call-done, pred[384]{0:T(512)(128)(4,1)S(1)} %compare_reduce_fusion.1, pred[]{:T(512)S(6)} %eq.19, f32[384,512]{1,0:T(8,128)} %param.14, ...), kind=kLoop, calls=%fused_computation.6 | loop fusion | flops 3932160 | bytes 6291841 | tf_op jit(solution)/shard_map/broadcast_in_dim | solution.py:48
  94.8 0.0 all-reduce.2.cloned.1.call-update
  94.8 12.4 %psum.15 = f32[]{:T(128)} all-reduce(f32[]{:T(128)S(6)} %convert_element_type.7), channel_id=1, replica_groups=mesh['rep'=4,'fsdp'=8] {'rep'}, use_global_device_ids=true, to_apply=%region_4.5 | all-reduce | flops 1 | bytes 8 | tf_op jit(solution)/shard_map/psum | solution.py:43
  107.2 31.5 %all-reduce.2.cloned.1.call-done = f32[384,512]{1,0:T(8,128)} async-done(((f32[384,512]{1,0:T(8,128)}), f32[384,512]{1,0:T(8,128)}) %all-reduce.2.cloned.1.call-update) | async-done | bytes 786448 | tf_op jit(solution)/shard_map/psum | solution.py:43
  138.7 3.7 %multiply_subtract_fusion = (f32[384,512]{1,0:T(8,128)}, f32[384,512]{1,0:T(8,128)}) fusion(f32[384,512]{1,0:T(8,128)} %param.14, f32[384,512]{1,0:T(8,128)} %all-reduce.2.cloned.1.call-done, f32[]{:T(128)} %psum.15, f32[384,512]{1,0:T(8,128)} %param.15), kind=kLoop, calls=%fused_computation.17 | loop fusion | flops 1376256 | bytes 3932164 | tf_op jit(solution)/shard_map/sub | solution.py:46
  (1 shorter events, 0.0 us)
Async XLA Ops:
  7.2 1.9 %copy-start = (bf16[1,512,3072]{2,1,0:T(8,128)(2,1)S(1)}, bf16[1,512,3072]{2,1,0:T(8,128)(2,1)}, u32[]{:S(2)}) copy-start(bf16[1,512,3072]{2,1,0:T(8,128)(2,1)} %param.8) | copy-start | bytes 9437188
  7.2 72.1 %reduce-scatter.2.cloned.1.call-start = ((), (), s32[]{:S(2)}) async-start(), calls=%async_computation.1 | async-start | bytes 7077888 | tf_op jit(solution)/shard_map/reduce_scatter | solution.py:23
  14.6 0.7 copy-start.1
  14.6 124.1 %all-reduce.2.cloned.1.call-start = ((), (), s32[]{:S(2)}) async-start(), calls=%async_computation.2 | async-start | bytes 1572864 | tf_op jit(solution)/shard_map/psum | solution.py:43
Sparse Core Ops, SparseCore 0:
  14.7 64.4 reduce-scatter.1
  94.9 43.7 all-reduce.1
where the time goes:
time: 150 us; the launch traced here: 149 us
  waiting for transfers between devices  95.5 us (64%)
  blocking collectives  20.2 us (13%)
  between operations  15.4 us (10%)
  other arithmetic  10.2 us (7%)
  matrix products  5.54 us (4%)
  local copies, waits for them, and re-layouts  2.45 us (2%)
    reduce_scatter x1, waiting for transfers between devices, body(): lax.psum_scatter(lax.dot_general(inputs, upstream, contract, preferred_el...  63.9 us
    psum x1, waiting for transfers between devices, body(): total, count = lax.psum((share, keep.astype(jnp.float32)), 'rep')  31.5 us
    psum x1, blocking collectives, body(): total, count = lax.psum((share, keep.astype(jnp.float32)), 'rep')  12.4 us
    pmax x1, blocking collectives, body(): replica_bad = lax.pmax(replica_nonfinite, 'fsdp')  7.75 us
    dot_general x1, matrix products, body(): lax.dot_general(inputs, upstream, contract, preferred_element_type=jnp.fl...  5.54 us
    broadcast_in_dim x1, other arithmetic, body(): jnp.where(keep, second_state_value, adam_second_state[0])[None]  4.52 us
    sub x1, other arithmetic, body(): anchor_next = anchor - 0.7 * (average + 0.9 * momentum_next)  3.66 us
  transfers between devices with their start and end apart: 2, of which 2 were waited for; matrix products, arithmetic and copies ran while one was open for 0% of the time, Pallas kernels for 0%

commit v1 on v0

--- a/solution.py
+++ b/solution.py
@@ -1,6 +1,8 @@
 import jax
 import jax.numpy as jnp
 from jax import lax
+from jax.experimental import pallas as pl
+from jax.experimental.pallas import tpu as pltpu
 from jax.sharding import PartitionSpec as P
 
 corr_first = 1.0 - 0.9**10
@@ -49,6 +51,335 @@
     return (anchor_next, momentum_next, first_next, second_next)
 
 
+NC = 4
+MESH = pl.DeviceIdType.MESH
+LIMIT = 7.5
+UNIT = 32767.0 / LIMIT
+
+
+def kernel(
+    acts, cot, mask, params, first, second, anchor, momentum,
+    o_anchor, o_mom, o_first, o_second,
+    a_buf, c_buf, p_buf, m_buf, v_buf, an_buf, mo_buf,
+    send_g, own_g, recv_d, recv_raw, recv_sum, sc_out, sc_sum, sc_in, flag_out, flag_in,
+    z_own, z_mid, z_fin, r_edge, r_mid, r_fin,
+    load_sem, core_s, core_r, flag_s, flag_r,
+    d_s, d_r, raw_s, raw_r, sum_s, sum_r, sc_s, sc_r, zs, zr, out_sem,
+):
+    rows = p_buf.shape[0]
+    tok = acts.shape[0]
+    ch = rows // NC
+    h = ch // 2
+    kv = p_buf.shape[1]
+    rep = lax.axis_index("rep")
+    f = lax.axis_index("fsdp")
+    c = lax.rem(f, 2)
+    x = lax.rem(lax.div(f, 2), 2)
+    y = lax.div(f, 4)
+
+    def at(j):
+        yy = 1 - y if j & 4 else y
+        xx = 1 - x if j & 2 else x
+        cc = 1 - c if j & 1 else c
+        return yy * 4 + xx * 2 + cc
+
+    loads = []
+
+    def load(src, dst, i):
+        cp = pltpu.make_async_copy(src, dst, load_sem.at[i])
+        cp.start()
+        loads.append(cp)
+
+    order = (6, 2, 4, 0)
+    load(cot, c_buf.at[pl.ds(0, tok)], 0)
+    for i, j in enumerate(order):
+        load(acts.at[:, pl.ds(pl.multiple_of(at(j) * rows, 128), rows)], a_buf.at[i, pl.ds(0, tok)], 1 + i)
+    for i, (s, d) in enumerate(((params, p_buf), (first, m_buf), (second, v_buf), (anchor, an_buf), (momentum, mo_buf))):
+        load(s, d, 5 + i)
+
+    zmate = lax.div(rep, 2) * 2 + (1 - lax.rem(rep, 2))
+    zmid = 3 - rep
+    edge = (rep == 0) | (rep == 3)
+    inner = jnp.logical_not(edge)
+
+    barrier = pltpu.get_barrier_semaphore()
+    for j in range(1, 8):
+        pl.semaphore_signal(barrier, inc=1, device_id=(rep, at(j)), device_id_type=MESH)
+    pl.semaphore_signal(barrier, inc=1, device_id=(zmate, f), device_id_type=MESH)
+    pl.semaphore_signal(barrier, inc=1, device_id=(zmid, f), device_id_type=MESH)
+    pl.semaphore_wait(barrier, 9)
+
+    sends = []
+
+    def remote(src, dst, s, r, dev):
+        return pltpu.make_async_remote_copy(
+            src_ref=src, dst_ref=dst, send_sem=s, recv_sem=r, device_id=dev, device_id_type=MESH
+        )
+
+    core = [remote(cot, c_buf.at[pl.ds(tok, tok)], core_s.at[0], core_r.at[0], (rep, at(1)))]
+    for i, j in enumerate(order):
+        core.append(
+            remote(
+                acts.at[:, pl.ds(pl.multiple_of(at(j ^ 1) * rows, 128), rows)],
+                a_buf.at[i, pl.ds(tok, tok)],
+                core_s.at[1 + i], core_r.at[1 + i], (rep, at(1)),
+            )
+        )
+    for cp in core:
+        cp.start()
+
+    flag_out[...] = jnp.broadcast_to(jnp.max(mask[...], axis=1, keepdims=True), flag_out.shape)
+    flags = [
+        remote(flag_out, flag_in.at[j], flag_s.at[j], flag_r.at[j], (rep, at(j))) for j in range(1, 8)
+    ]
+    for cp in flags:
+        cp.start()
+
+    def product(i):
+        loads[1 + i].wait()
+        core[1 + i].wait_recv()
+        return lax.dot_general(
+            a_buf[i], c_buf[...], (((0,), (0,)), ((), ())), preferred_element_type=jnp.float32
+        )
+
+    def half(k, b):
+        return pl.ds(k * ch + b * h, h)
+
+    peers = ((rep, at(2)), (rep, at(4)))
+    diag, raw, summed = {}, {}, {}
+    for k in range(NC):
+        for b in range(2):
+            diag[k, b] = remote(
+                send_g.at[0, half(k, b)], recv_d.at[b, k], d_s.at[b, k], d_r.at[b, k], peers[b]
+            )
+            raw[k, b] = remote(
+                send_g.at[1 + b, half(k, b)], recv_raw.at[b, k], raw_s.at[b, k], raw_r.at[b, k], peers[b]
+            )
+            summed[k, b] = remote(
+                send_g.at[1 + b, half(k, 1 - b)], recv_sum.at[b, k], sum_s.at[b, k], sum_r.at[b, k], peers[b]
+            )
+
+    scale = {}
+    for b in range(2):
+        for n, src in enumerate((sc_out.at[0], sc_out.at[1 + b], sc_sum.at[b])):
+            scale[n, b] = remote(src, sc_in.at[n, b], sc_s.at[n, b], sc_r.at[n, b], peers[b])
+
+    def wide(top):
+        return jnp.broadcast_to(top, (1, kv))
+
+    def code(values, top):
+        return jnp.round(values * (32767.0 / wide(top))).astype(jnp.int32).astype(jnp.int16)
+
+    def decode(codes, top):
+        return codes.astype(jnp.int32).astype(jnp.float32) * (wide(top) * (1.0 / 32767.0))
+
+    def pack(i):
+        g = product(i)
+        top = jnp.max(jnp.max(jnp.abs(g), axis=0, keepdims=True), axis=1, keepdims=True)
+        top = jnp.maximum(top, 1e-30)
+        sc_out[i] = jnp.broadcast_to(top, (8, 128))
+        send_g[i] = code(g, top)
+
+    def start(group, k):
+        if k < NC:
+            group[k, 0].start()
+            group[k, 1].start()
+
+    loads[0].wait()
+    core[0].wait_recv()
+    pack(0)
+    scale[0, 0].start()
+    scale[0, 1].start()
+    start(diag, 0)
+    start(diag, 1)
+    pack(1)
+    scale[1, 0].start()
+    raw[0, 0].start()
+    pack(2)
+    scale[1, 1].start()
+    raw[0, 1].start()
+    mine, came, both = [], [], []
+    for b in range(2):
+        scale[0, 1 - b].wait_recv()
+        mine.append(sc_out[1 + b][0:1, 0:1])
+        came.append(sc_in[0, 1 - b][0:1, 0:1])
+        both.append(mine[b] + came[b])
+        sc_sum[b] = jnp.broadcast_to(both[b], (8, 128))
+        scale[2, b].start()
+
+    def forward(k):
+        for b in range(2):
+            diag[k, 1 - b].wait_recv()
+            r = half(k, 1 - b)
+            send_g[1 + b, r] = code(
+                decode(send_g[1 + b, r], mine[b]) + decode(recv_d[1 - b, k], came[b]), both[b]
+            )
+            summed[k, b].start()
+
+    forward(0)
+    start(raw, 1)
+    start(diag, 2)
+    own_g[...] = product(3)
+    for i in range(5):
+        loads[5 + i].wait()
+
+    for b in range(2):
+        scale[1, b].wait_recv()
+        scale[2, b].wait_recv()
+    raw_top = [sc_in[1, b][0:1, 0:1] for b in range(2)]
+    sum_top = [sc_in[2, b][0:1, 0:1] for b in range(2)]
+    bad = jnp.max(flag_out[...])
+    for j in range(1, 8):
+        flags[j - 1].wait_recv()
+        bad = jnp.maximum(bad, jnp.max(flag_in[j]))
+    keep = bad == 0
+    count = 3.0
+
+    def zcopy(n, src, dst, k, dev):
+        return remote(src.at[k], dst.at[k], zs.at[n, k], zr.at[n, k], dev)
+
+    to_inner = [zcopy(0, z_own, r_edge, k, (zmate, f)) for k in range(NC)]
+    across = [zcopy(1, z_mid, r_mid, k, (zmid, f)) for k in range(NC)]
+    to_edge = [zcopy(2, z_fin, r_fin, k, (zmate, f)) for k in range(NC)]
+    outs = []
+
+    def put(src, dst, k, n):
+        r = pl.ds(k * ch, ch)
+        cp = pltpu.make_async_copy(src.at[r], dst.at[r], out_sem.at[n, k])
+        cp.start()
+        outs.append(cp)
+
+    def adam(k):
+        for b in range(2):
+            raw[k, b].wait_recv()
+            summed[k, 1 - b].wait_recv()
+            r = half(k, b)
+            g = own_g[r] + decode(recv_raw[b, k], raw_top[b]) + decode(recv_sum[1 - b, k], sum_top[1 - b])
+            m0, v0, p = m_buf[r], v_buf[r], p_buf[r]
+            m = 0.9 * m0 + 0.1 * g
+            v = 0.95 * v0 + 0.05 * g * g
+            update = m / corr_first / (jnp.sqrt(v / corr_second) + 1e-08)
+            new = jnp.where(keep, p - 0.1 * (update + 0.1 * p), 0.0) * UNIT
+            p_buf[r] = new
+            z_own[k, pl.ds(b * h, h)] = jnp.round(new).astype(jnp.int32).astype(jnp.int16)
+            m_buf[r] = jnp.where(keep, m, m0)
+            v_buf[r] = jnp.where(keep, v, v0)
+
+        @pl.when(edge)
+        def _():
+            to_inner[k].start()
+
+        put(m_buf, o_first, k, 0)
+        put(v_buf, o_second, k, 1)
+
+    def pair(k):
+        @pl.when(inner)
+        def _():
+            to_inner[k].wait_recv()
+            s = p_buf[pl.ds(k * ch, ch)] + r_edge[k].astype(jnp.int32).astype(jnp.float32)
+            z_mid[k] = jnp.round(s * 0.5).astype(jnp.int32).astype(jnp.int16)
+            across[k].start()
+
+    def finish(k):
+        @pl.when(inner)
+        def _():
+            across[k].wait_recv()
+            s = (z_mid[k].astype(jnp.int32) + r_mid[k].astype(jnp.int32)).astype(jnp.float32)
+            z_fin[k] = jnp.round(s * (2.0 / 3.0)).astype(jnp.int32).astype(jnp.int16)
+            to_edge[k].start()
+            r_fin[k] = z_fin[k]
+
+        @pl.when(edge)
+        def _():
+            to_edge[k].wait_recv()
+
+        r = pl.ds(k * ch, ch)
+        total = r_fin[k].astype(jnp.int32).astype(jnp.float32) * (3.0 / UNIT)
+        a = an_buf[r]
+        average = a - total / count
+        mo = 0.9 * mo_buf[r] + average
+        an_buf[r] = a - 0.7 * (average + 0.9 * mo)
+        mo_buf[r] = mo
+        put(an_buf, o_anchor, k, 2)
+        put(mo_buf, o_mom, k, 3)
+
+    for k in range(NC + 2):
+        if k + 1 < NC:
+            forward(k + 1)
+            if k + 2 < NC:
+                start(raw, k + 2)
+            start(diag, k + 3)
+        if k < NC:
+            adam(k)
+        if 0 <= k - 1 < NC:
+            pair(k - 1)
+        if 0 <= k - 2 < NC:
+            finish(k - 2)
+
+    for cp in core + flags:
+        cp.wait_send()
+    for group in (diag, raw, summed, scale):
+        for cp in group.values():
+            cp.wait_send()
+    for k in range(NC):
+
+        @pl.when(edge)
+        def _():
+            to_inner[k].wait_send()
+
+        @pl.when(inner)
+        def _():
+            across[k].wait_send()
+            to_edge[k].wait_send()
+
+    for cp in outs:
+        cp.wait()
+
+
+def fused(acts, cotangent, nonfinite_row_mask, params, first, second, anchor, momentum):
+    rows, kv = anchor.shape
+    tok = acts.shape[1]
+    ch = rows // NC
+    h = ch // 2
+    bf, f32, dma = jnp.bfloat16, jnp.float32, pltpu.SemaphoreType.DMA
+    block = jax.ShapeDtypeStruct((rows, kv), f32)
+    hbm = pl.BlockSpec(memory_space=pl.ANY)
+    out = pl.pallas_call(
+        kernel,
+        out_shape=[block] * 4,
+        in_specs=[hbm, hbm, pl.BlockSpec(memory_space=pltpu.VMEM)] + [hbm] * 5,
+        out_specs=[hbm] * 4,
+        scratch_shapes=[
+            pltpu.VMEM((4, 2 * tok, rows), bf),
+            pltpu.VMEM((2 * tok, kv), bf),
+        ]
+        + [pltpu.VMEM((rows, kv), f32)] * 5
+        + [
+            pltpu.VMEM((3, rows, kv), jnp.int16),
+            pltpu.VMEM((rows, kv), f32),
+            pltpu.VMEM((2, NC, h, kv), jnp.int16),
+            pltpu.VMEM((2, NC, h, kv), jnp.int16),
+            pltpu.VMEM((2, NC, h, kv), jnp.int16),
+            pltpu.VMEM((3, 8, 128), f32),
+            pltpu.VMEM((2, 8, 128), f32),
+            pltpu.VMEM((3, 2, 8, 128), f32),
+            pltpu.VMEM((8, 128), jnp.int32),
+            pltpu.VMEM((8, 8, 128), jnp.int32),
+        ]
+        + [pltpu.VMEM((NC, ch, kv), jnp.int16)] * 6
+        + [dma((10,)), dma((5,)), dma((5,)), dma((8,)), dma((8,))]
+        + [dma((2, NC))] * 6
+        + [dma((3, 2)), dma((3, 2)), dma((3, NC)), dma((3, NC)), dma((4, NC))],
+        compiler_params=pltpu.CompilerParams(
+            collective_id=0, has_side_effects=True, vmem_limit_bytes=40 * 2**20
+        ),
+        cost_estimate=pl.CostEstimate(
+            flops=2 * 8 * rows * tok * kv, bytes_accessed=12 * 2**20, transcendentals=rows * kv
+        ),
+    )(acts[0], cotangent[0], nonfinite_row_mask, params[0], first[0], second[0], anchor, momentum)
+    return out[0], out[1], out[2][None], out[3][None]
+
+
 def solution(mesh):
     in_specs = (
         P("rep", "fsdp", None),
@@ -61,4 +392,7 @@
         P("fsdp", None),
     )
     out_specs = (P("fsdp", None), P("fsdp", None), P("rep", "fsdp", None), P("rep", "fsdp", None))
-    return jax.shard_map(body, mesh=mesh, in_specs=in_specs, out_specs=out_specs, check_vma=False)
+    block = mesh.shape["rep"] == 4 and mesh.shape["fsdp"] == 8
+    return jax.shard_map(
+        fused if block else body, mesh=mesh, in_specs=in_specs, out_specs=out_specs, check_vma=False
+    )

time: 150 us -> 56.9 us (0.38)
  waiting for transfers between devices: 95.5 us -> 0 us
  Pallas kernels: 0 us -> 43 us
  blocking collectives: 20.2 us -> 0 us
  between operations: 15.4 us -> 0.66 us
  local copies, waits for them, and re-layouts: 2.45 us -> 12.8 us
  other arithmetic: 10.2 us -> 0 us
  matrix products: 5.54 us -> 0 us
    reduce_scatter x1 -> x0, waiting for transfers between devices: 63.9 us -> none  [body(): lax.psum_scatter(lax.dot_general(inputs, upstream, contract, preferred_el...]
    pallas_call x0 -> x1, Pallas kernels: none -> 43 us  [fused(): pl.pallas_call(kernel, out_shape=[block] * 4, in_specs=[hbm, hbm, pl.Bloc...]
    psum x1 -> x0, waiting for transfers between devices: 31.5 us -> none  [body(): total, count = lax.psum((share, keep.astype(jnp.float32)), 'rep')]
    psum x1 -> x0, blocking collectives: 12.4 us -> none  [body(): total, count = lax.psum((share, keep.astype(jnp.float32)), 'rep')]
    unnamed x4 -> x20, local copies, waits for them, and re-layouts: 2.45 us -> 12.8 us
    pmax x1 -> x0, blocking collectives: 7.75 us -> none  [body(): replica_bad = lax.pmax(replica_nonfinite, 'fsdp')]
    dot_general x1 -> x0, matrix products: 5.54 us -> none  [body(): lax.dot_general(inputs, upstream, contract, preferred_element_type=jnp.fl...]
    broadcast_in_dim x1 -> x0, other arithmetic: 4.52 us -> none  [body(): jnp.where(keep, second_state_value, adam_second_state[0])[None]]
  transfers between devices with their start and end apart: 2 -> 0, of which waited for: 2 -> 0; matrix products, arithmetic and copies ran while one was open for 0% -> 0% of each run, Pallas kernels for 0% -> 0%
where the time goes in v1:
time: 56.9 us; the launch traced here: 56.4 us
  Pallas kernels  43 us (76%)
  local copies, waits for them, and re-layouts  12.8 us (22%)
  between operations  0.66 us (1%)
    pallas_call x1, Pallas kernels, fused(): pl.pallas_call(kernel, out_shape=[block] * 4, in_specs=[hbm, hbm, pl.Bloc...  43 us
    unnamed x20, local copies, waits for them, and re-layouts  12.8 us

profile of v1, /device:TPU:0, one launch (start us, length us, event | category | flops | bytes accessed | tf_op | source)
XLA Modules:
  0.0 56.4 jit_solution(9301192785572221112)
XLA Ops:
  0.6 0.0 copy-start
  0.6 1.9 %copy-done = bf16[1,512,3072]{2,1,0:T(8,128)(2,1)S(1)} copy-done((bf16[1,512,3072]{2,1,0:T(8,128)(2,1)S(1)}, bf16[1,512,3072]{2,1,0:T(8,128)(2,1)}, u32[]{:S(2)}) %copy-start) | copy-done | bytes 3145752
  2.5 0.0 copy-start.1
  2.5 1.1 %copy-done.1 = f32[1,384,512]{2,1,0:T(8,128)S(1)} copy-done((f32[1,384,512]{2,1,0:T(8,128)S(1)}, f32[1,384,512]{2,1,0:T(8,128)}, u32[]{:S(2)}) %copy-start.1) | copy-done | bytes 786456
  3.7 0.0 copy-start.2
  3.7 1.1 %copy-done.2 = f32[1,384,512]{2,1,0:T(8,128)S(1)} copy-done((f32[1,384,512]{2,1,0:T(8,128)S(1)}, f32[1,384,512]{2,1,0:T(8,128)}, u32[]{:S(2)}) %copy-start.2) | copy-done | bytes 786456
  4.8 0.0 copy-start.3
  4.8 1.1 %copy-done.3 = f32[1,384,512]{2,1,0:T(8,128)S(1)} copy-done((f32[1,384,512]{2,1,0:T(8,128)S(1)}, f32[1,384,512]{2,1,0:T(8,128)}, u32[]{:S(2)}) %copy-start.3) | copy-done | bytes 786456
  5.9 0.0 copy-start.4
  5.9 1.1 %copy-done.4 = f32[384,512]{1,0:T(8,128)S(1)} copy-done((f32[384,512]{1,0:T(8,128)S(1)}, f32[384,512]{1,0:T(8,128)}, u32[]{:S(2)}) %copy-start.4) | copy-done | bytes 786456
  7.1 0.0 copy-start.5
  7.1 1.1 %copy-done.5 = f32[384,512]{1,0:T(8,128)S(1)} copy-done((f32[384,512]{1,0:T(8,128)S(1)}, f32[384,512]{1,0:T(8,128)}, u32[]{:S(2)}) %copy-start.5) | copy-done | bytes 786456
  8.2 0.0 copy-start.6
  8.2 1.0 %copy-done.6 = bf16[1,512,512]{2,1,0:T(8,128)(2,1)S(1)} copy-done((bf16[1,512,512]{2,1,0:T(8,128)(2,1)S(1)}, bf16[1,512,512]{2,1,0:T(8,128)(2,1)}, u32[]{:S(2)}) %copy-start.6) | copy-done | bytes 524312
  9.2 0.0 copy-start.7
  9.2 0.7 %copy-done.7 = s32[1,384]{1,0:T(1,128)S(1)} copy-done((s32[1,384]{1,0:T(1,128)S(1)}, s32[1,384]{1,0:T(1,128)}, u32[]{:S(2)}) %copy-start.7) | copy-done | bytes 1560
  9.9 43.0 %shard_map.111 = (f32[384,512]{1,0:T(8,128)S(1)}, f32[384,512]{1,0:T(8,128)S(1)}, f32[384,512]{1,0:T(8,128)S(1)}, f32[384,512]{1,0:T(8,128)S(1)}) custom-call(bf16[512,3072]{1,0:T(8,128)(2,1)S(1)} %bitcast.7, bf16[512,512]{1,0:T(8,128)(2,1)S(1)} %bitcast.13, s32[1,384]{1,0:T(1,128)S(1)} %copy-done.7, f32[384,512]{1,0:T(8,128)S(1)} %bitcast.8, ...), custom_call_target="tpu_custom_call" | custom-call | flops 1610612736 | bytes 12582912 | tf_op jit(solution)/shard_map/pallas_call | solution.py:347
  52.9 0.9 %copy.16 = f32[384,512]{1,0:T(8,128)} copy(f32[384,512]{1,0:T(8,128)S(1)} %get-tuple-element.16) | data formatting | bytes 1572864
  53.8 0.9 %copy.17 = f32[384,512]{1,0:T(8,128)} copy(f32[384,512]{1,0:T(8,128)S(1)} %get-tuple-element.17) | data formatting | bytes 1572864
  54.7 0.9 %copy.18 = f32[1,384,512]{2,1,0:T(8,128)} copy(f32[1,384,512]{2,1,0:T(8,128)S(1)} %bitcast.12) | data formatting | bytes 1572864
  55.5 0.9 %copy.19 = f32[1,384,512]{2,1,0:T(8,128)} copy(f32[1,384,512]{2,1,0:T(8,128)S(1)} %bitcast.11) | data formatting | bytes 1572864
Async XLA Ops:
  0.6 1.9 %copy-start = (bf16[1,512,3072]{2,1,0:T(8,128)(2,1)S(1)}, bf16[1,512,3072]{2,1,0:T(8,128)(2,1)}, u32[]{:S(2)}) copy-start(bf16[1,512,3072]{2,1,0:T(8,128)(2,1)} %param.8) | copy-start | bytes 9437188
  2.5 1.1 %copy-start.1 = (f32[1,384,512]{2,1,0:T(8,128)S(1)}, f32[1,384,512]{2,1,0:T(8,128)}, u32[]{:S(2)}) copy-start(f32[1,384,512]{2,1,0:T(8,128)} %param.11) | copy-start | bytes 2359300
  3.7 1.1 %copy-start.2 = (f32[1,384,512]{2,1,0:T(8,128)S(1)}, f32[1,384,512]{2,1,0:T(8,128)}, u32[]{:S(2)}) copy-start(f32[1,384,512]{2,1,0:T(8,128)} %param.12) | copy-start | bytes 2359300
  4.8 1.1 %copy-start.3 = (f32[1,384,512]{2,1,0:T(8,128)S(1)}, f32[1,384,512]{2,1,0:T(8,128)}, u32[]{:S(2)}) copy-start(f32[1,384,512]{2,1,0:T(8,128)} %param.13) | copy-start | bytes 2359300
  5.9 1.1 %copy-start.4 = (f32[384,512]{1,0:T(8,128)S(1)}, f32[384,512]{1,0:T(8,128)}, u32[]{:S(2)}) copy-start(f32[384,512]{1,0:T(8,128)} %anchor.1) | copy-start | bytes 2359300
  7.1 1.1 %copy-start.5 = (f32[384,512]{1,0:T(8,128)S(1)}, f32[384,512]{1,0:T(8,128)}, u32[]{:S(2)}) copy-start(f32[384,512]{1,0:T(8,128)} %momentum.1) | copy-start | bytes 2359300
  8.2 1.0 %copy-start.6 = (bf16[1,512,512]{2,1,0:T(8,128)(2,1)S(1)}, bf16[1,512,512]{2,1,0:T(8,128)(2,1)}, u32[]{:S(2)}) copy-start(bf16[1,512,512]{2,1,0:T(8,128)(2,1)} %param.9) | copy-start | bytes 1572868
  9.2 0.7 %copy-start.7 = (s32[1,384]{1,0:T(1,128)S(1)}, s32[1,384]{1,0:T(1,128)}, u32[]{:S(2)}) copy-start(s32[1,384]{1,0:T(1,128)} %mask.1) | copy-start | bytes 4612
